TPU v7x, 512 devices: a whole 4x4x16 slice. The times are simulated.
512 devices in a mesh: prow: 16 (over z), pcol: 32 (over y, x, core).
Axes of the slice: x: 4, y: 4, z: 16, core: 2. Of those that a mesh axis runs over, the one named last changes fastest.
Arguments:
- matrix: float32 [2, 16, 256, 32, 256], P(None, 'prow', None, 'pcol'), may hold values from -6 to 6, as said below
Outputs:
- factored: float32 [2, 16, 256, 32, 256], P(None, 'prow', None, 'pcol')
Inputs may be any that keep to these rules, and one draw needn't show every extreme that they name: `matrix`: in the first 3 diagonal blocks every diagonal entry lies between 1.3 and 3.2, and diag(1/d) times the off-diagonal part of each such block has spectral norm below about 0.7.
All inputs are finite; a program needn't handle non-finite values.
Results may differ from a plain program's by a relative error of at most 0.0001.
Values sent between devices are 32-bit elements; how exact they have to be, the bound alone decides.
A program may use at most 64 MiB of HBM per device.

v0:
```python
import jax
import jax.numpy as jnp
from jax import lax
from jax.sharding import PartitionSpec as P

PANELS = 3


def from_root(block, axis, owner):
    block = jnp.where(lax.axis_index(axis) == owner, block, jnp.zeros_like(block))
    return lax.psum(block, axis)


def invert(block):
    scales = 1.0 / jnp.diagonal(block)
    first = 2.0 * jnp.diag(scales) - scales[:, None] * block * scales[None, :]
    inner = jnp.dot(block, first, precision=lax.Precision.HIGHEST)
    return 2.0 * first - jnp.dot(first, inner, precision=lax.Precision.HIGHEST)


def blockwise(left, right):
    return jnp.einsum("rij,jk->rik", left, right, precision=lax.Precision.HIGHEST)


def empty_like(block):
    return jnp.zeros_like(block)


def body(matrix):
    shape = matrix.shape
    tile = matrix.reshape(shape[0], shape[2], shape[4])
    my_row = lax.axis_index("prow")
    my_col = lax.axis_index("pcol")
    row_count = lax.axis_size("prow")
    block_row = (jnp.arange(shape[0], dtype=jnp.int32) * row_count + my_row)[:, None, None]
    for panel in range(PANELS):
        below = block_row > panel
        owns_pivot = (my_row == panel) & (my_col == panel)
        local_inverse = lax.cond(owns_pivot, invert, empty_like, tile[0])
        inverse = from_root(local_inverse, "prow", panel)

        def make_factors(operands):
            return jnp.where(below, blockwise(operands[0], operands[1]), 0.0)

        def no_factors(operands):
            return jnp.zeros_like(operands[0])

        local_factors = lax.cond(my_col == panel, make_factors, no_factors, (tile, inverse))
        factors = from_root(local_factors, "pcol", panel)
        pivot_row = from_root(tile[0], "prow", panel)
        update = blockwise(factors, pivot_row)
        tile = jnp.where(below & (my_col > panel), tile - update, tile)
        column = jnp.where(below, factors, jnp.where(block_row == panel, inverse[None], tile))
        tile = jnp.where(my_col == panel, column, tile)
    return tile.reshape(shape)


def solution(mesh):
    return jax.shard_map(
        body,
        mesh=mesh,
        in_specs=(P(None, "prow", None, "pcol", None),),
        out_specs=P(None, "prow", None, "pcol", None),
        check_vma=False,
    )
```

profile of v0, /device:TPU:1, one launch (start us, length us, event | category | flops | bytes accessed | tf_op | source)
XLA Modules:
  0.0 845.4 jit_solution(9275710195881586795)
XLA Ops:
  6.5 1.1 slice.13
  7.7 0.8 broadcast_select_fusion.7
  8.6 0.0 all-reduce.10.cloned.1.call-start
  8.7 1.0 copy-done
  9.7 132.9 %all-reduce.20.cloned.1.call-done = (f32[256,256]{1,0:T(8,128)}, f32[256,256]{1,0:T(8,128)}) async-done(((f32[256,256]{1,0:T(8,128)}, f32[256,256]{1,0:T(8,128)}), (f32[256,256]{1,0:T(8,128)}, f32[256,256]{1,0:T(8,128)})) %all-reduce.20.cloned.1.call-update) | async-done | bytes 524304 | tf_op jit(solution)/shard_map/psum | solution.py:11
  142.6 0.8 broadcast_select_fusion.2
  143.5 142.9 %all-reduce.10.cloned.1.call-done = f32[2,256,256]{2,1,0:T(8,128)} async-done(((f32[2,256,256]{2,1,0:T(8,128)}), f32[2,256,256]{2,1,0:T(8,128)}) %all-reduce.10.cloned.1.call-update) | async-done | bytes 524304 | tf_op jit(solution)/shard_map/psum | solution.py:11
  286.5 1.8 select_select_fusion.1
  288.3 0.7 broadcast_select_fusion.5
  289.1 0.7 broadcast_select_fusion.6
  289.9 127.3 %all-reduce.18.cloned.1.call-done = (f32[256,256]{1,0:T(8,128)}, f32[256,256]{1,0:T(8,128)}) async-done(((f32[256,256]{1,0:T(8,128)}, f32[256,256]{1,0:T(8,128)}), (f32[256,256]{1,0:T(8,128)}, f32[256,256]{1,0:T(8,128)})) %all-reduce.18.cloned.1.call-update) | async-done | bytes 524304 | tf_op jit(solution)/shard_map/psum | solution.py:11
  417.1 1.5 conditional.9
  417.2 1.5 convolution_select_fusion.1
  418.7 0.8 broadcast_select_fusion.1
  419.6 0.0 all-reduce.16.cloned.1.call-start
  419.6 141.3 %all-reduce.12.cloned.1.call-done = f32[2,256,256]{2,1,0:T(8,128)} async-done(((f32[2,256,256]{2,1,0:T(8,128)}), f32[2,256,256]{2,1,0:T(8,128)}) %all-reduce.12.cloned.1.call-update) | async-done | bytes 524304 | tf_op jit(solution)/shard_map/psum | solution.py:11
  560.9 1.8 select_select_fusion
  562.8 0.7 broadcast_select_fusion.3
  563.5 0.7 broadcast_select_fusion.4
  564.3 127.3 %all-reduce.16.cloned.1.call-done = (f32[256,256]{1,0:T(8,128)}, f32[256,256]{1,0:T(8,128)}) async-done(((f32[256,256]{1,0:T(8,128)}, f32[256,256]{1,0:T(8,128)}), (f32[256,256]{1,0:T(8,128)}, f32[256,256]{1,0:T(8,128)})) %all-reduce.16.cloned.1.call-update) | async-done | bytes 524304 | tf_op jit(solution)/shard_map/psum | solution.py:11
  691.7 0.8 broadcast_select_fusion
  692.6 142.8 %all-reduce.14.cloned.1.call-done = f32[2,256,256]{2,1,0:T(8,128)} async-done(((f32[2,256,256]{2,1,0:T(8,128)}), f32[2,256,256]{2,1,0:T(8,128)}) %all-reduce.14.cloned.1.call-update) | async-done | bytes 524304 | tf_op jit(solution)/shard_map/psum | solution.py:11
  835.4 1.8 select_bitcast_fusion
  837.2 1.3 copy.5
  (45 shorter events, 0.7 us)
Async XLA Ops:
  6.5 136.0 %all-reduce.20.cloned.1.call-start = ((), (), s32[]{:S(2)}) async-start(), calls=%async_computation.5 | async-start | bytes 1048576 | tf_op jit(solution)/shard_map/psum | solution.py:11
  8.6 1.0 copy-start
  8.6 277.8 %all-reduce.10.cloned.1.call-start = ((), (), s32[]{:S(2)}) async-start(), calls=%async_computation | async-start | bytes 1048576 | tf_op jit(solution)/shard_map/psum | solution.py:11
  143.4 143.0 %copy-start.1 = (f32[256,256]{1,0:T(8,128)S(1)}, f32[256,256]{1,0:T(8,128)}, u32[]{:S(2)}) copy-start(f32[256,256]{1,0:T(8,128)} %get-tuple-element.66) | copy-start | bytes 786436
  143.4 143.0 %copy-start.4 = (f32[256,256]{1,0:T(8,128)S(1)}, f32[256,256]{1,0:T(8,128)}, u32[]{:S(2)}) copy-start(f32[256,256]{1,0:T(8,128)} %get-tuple-element.67) | copy-start | bytes 786436
  143.4 273.7 %all-reduce.18.cloned.1.call-start = ((), (), s32[]{:S(2)}) async-start(), calls=%async_computation.4 | async-start | bytes 1048576 | tf_op jit(solution)/shard_map/psum | solution.py:11
  289.8 271.1 %all-reduce.12.cloned.1.call-start = ((), (), s32[]{:S(2)}) async-start(), calls=%async_computation.1 | async-start | bytes 1048576 | tf_op jit(solution)/shard_map/psum | solution.py:11
  419.5 141.4 %copy-start.2 = (f32[256,256]{1,0:T(8,128)S(1)}, f32[256,256]{1,0:T(8,128)}, u32[]{:S(2)}) copy-start(f32[256,256]{1,0:T(8,128)} %get-tuple-element.64) | copy-start | bytes 786436
  419.5 141.4 %copy-start.5 = (f32[256,256]{1,0:T(8,128)S(1)}, f32[256,256]{1,0:T(8,128)}, u32[]{:S(2)}) copy-start(f32[256,256]{1,0:T(8,128)} %get-tuple-element.65) | copy-start | bytes 786436
  419.6 272.1 %all-reduce.16.cloned.1.call-start = ((), (), s32[]{:S(2)}) async-start(), calls=%async_computation.3 | async-start | bytes 1048576 | tf_op jit(solution)/shard_map/psum | solution.py:11
  564.3 271.1 %all-reduce.14.cloned.1.call-start = ((), (), s32[]{:S(2)}) async-start(), calls=%async_computation.2 | async-start | bytes 1048576 | tf_op jit(solution)/shard_map/psum | solution.py:11
  692.5 142.9 %copy-start.3 = (f32[256,256]{1,0:T(8,128)S(1)}, f32[256,256]{1,0:T(8,128)}, u32[]{:S(2)}) copy-start(f32[256,256]{1,0:T(8,128)} %get-tuple-element.62) | copy-start | bytes 786436
  692.5 142.9 %copy-start.6 = (f32[256,256]{1,0:T(8,128)S(1)}, f32[256,256]{1,0:T(8,128)}, u32[]{:S(2)}) copy-start(f32[256,256]{1,0:T(8,128)} %get-tuple-element.63) | copy-start | bytes 786436
Sparse Core Ops, SparseCore 0:
  9.7 132.7 all-reduce.19
  146.0 140.3 all-reduce.9
  289.9 127.1 all-reduce.17
  420.5 140.3 all-reduce.11
  564.4 127.1 all-reduce.15
  695.0 140.3 all-reduce.13
where the time goes:
time: 846 us; the launch traced here: 845 us
  waiting for transfers between devices  815 us (96%)
  between operations  13.7 us (2%)
    psum x6, waiting for transfers between devices, from_root(): return lax.psum(block, axis)  814 us
  transfers between devices with their start and end apart: 6, of which 6 were waited for; matrix products, arithmetic and copies ran while one was open for 0% of the time, Pallas kernels for 0%

commit v1 on v0

v1 whole, which is shorter than its diff:
```python
import functools

import jax
import jax.numpy as jnp
from jax import lax
from jax.experimental import pallas as pl
from jax.experimental.pallas import tpu as pltpu
from jax.sharding import PartitionSpec as P

B = 256
PANELS = 3
NP = 16
NQ = 32
NC = NQ // 2
S = B // NQ
CHUNKS = 8
CR = B // CHUNKS
MESH = pl.DeviceIdType.MESH


def split(value):
    high = value.astype(jnp.bfloat16)
    return high, (value - high.astype(jnp.float32)).astype(jnp.bfloat16)


def dot3(left, right):
    dot = functools.partial(jnp.dot, preferred_element_type=jnp.float32)
    return dot(left[0], right[0]) + (dot(left[0], right[1]) + dot(left[1], right[0]))


def invert(block):
    row = lax.broadcasted_iota(jnp.int32, (B, B), 0)
    col = lax.broadcasted_iota(jnp.int32, (B, B), 1)
    eye = row == col
    diagonal = jnp.where(eye, block, 0.0)
    down = 1.0 / jnp.sum(diagonal, axis=1, keepdims=True)
    across = 1.0 / jnp.sum(diagonal, axis=0, keepdims=True)
    first = jnp.where(eye, 2.0 * down, 0.0) - down * block * across
    parts = split(first)
    inner = dot3(split(block), parts)
    return 2.0 * first - dot3(parts, split(inner))


def kernel(
    x_ref,
    out_ref,
    rs,
    rows,
    hs,
    head,
    cols,
    fact,
    upper,
    sc_send,
    sc_recv,
    ra_send,
    ra_recv,
    hz_send,
    hz_recv,
    ha_send,
    ha_recv,
    zu_send,
    zd_send,
    z_recv,
    cc_send,
    cc_recv,
):
    p = lax.axis_index("prow")
    q = lax.axis_index("pcol")
    core = lax.rem(q, 2)
    chip = q // 2
    partner = q + 1 - 2 * core

    def remote(src, dst, send, recv, row, col):
        return pltpu.make_async_remote_copy(
            src_ref=src, dst_ref=dst, send_sem=send, recv_sem=recv, device_id=(row, col), device_id_type=MESH
        )

    def mine(t):
        return pl.ds(pl.multiple_of((lax.rem(t, 2) * NC + t // 2) * S, S), S)

    barrier = pltpu.get_barrier_semaphore()

    @pl.loop(1, NQ)
    def _(j):
        pl.semaphore_signal(barrier, inc=1, device_id=(p, lax.rem(q + j, NQ)), device_id_type=MESH)

    @pl.loop(1, NP)
    def _(j):
        pl.semaphore_signal(barrier, inc=1, device_id=(lax.rem(p + j, NP), q), device_id_type=MESH)

    pl.semaphore_wait(barrier, NQ - 1 + NP - 1)

    def scatter(j):
        t = lax.rem(q + j, NQ)
        return remote(x_ref.at[:, mine(t)], rs.at[q], sc_send.at[j], sc_recv.at[q], p, t)

    @pl.when(q < PANELS)
    def _():
        rs[q] = x_ref[:, mine(q)]

        @pl.loop(1, NQ)
        def _(j):
            scatter(j).start()

    for k in range(PANELS):

        @pl.when(q != k)
        def _():
            remote(x_ref.at[:, pl.ds(0, S)], rs.at[k], sc_send.at[0], sc_recv.at[k], p, partner).wait_recv()

    def head_along(j):
        return remote(rs.at[:, 0], hs.at[p], hz_send.at[j], hz_recv.at[p], lax.rem(p + j, NP), q)

    @pl.when(p < PANELS)
    def _():
        hs[p] = rs[:, 0]

        @pl.loop(1, NP)
        def _(j):
            head_along(j).start()

    def gather(src, dst, send, recv, j):
        return remote(src, dst.at[core, chip], send.at[j], recv.at[chip], p, lax.rem(q + 2 * j, NQ))

    rows[core, chip] = rs[...]

    @pl.loop(1, NC)
    def _(j):
        gather(rs, rows, ra_send, ra_recv, j).start()

    for k in range(PANELS):

        @pl.when(p != k)
        def _():
            remote(rs.at[:, 0], hs.at[k], hz_send.at[0], hz_recv.at[k], lax.rem(p + 1, NP), q).wait_recv()

    head[core, chip] = hs[...]

    @pl.loop(1, NC)
    def _(j):
        gather(hs, head, ha_send, ha_recv, j).start()

    @pl.when(p < PANELS)
    def _():
        cols[p] = x_ref[0]

    def chunk(i):
        k = lax.rem(i, PANELS)
        c = i // PANELS
        odd = lax.rem(c, 2)
        reach = (1 - odd) * (11 - c // 2) + odd * (4 + c // 2)
        away = lax.rem(p - k + NP, NP)
        piece = cols.at[k, pl.ds(pl.multiple_of(c * CR, CR), CR)]
        up = remote(piece, piece, zu_send.at[i], z_recv.at[i], lax.rem(p + 1, NP), q)
        down = remote(piece, piece, zd_send.at[i], z_recv.at[i], lax.rem(p + NP - 1, NP), q)
        goes_up = away < reach
        goes_down = (away == 0) | (away > reach + 1)
        return away, up, down, goes_up, goes_down

    @pl.loop(0, PANELS * CHUNKS)
    def _(i):
        away, up, down, goes_up, goes_down = chunk(i)

        @pl.when(away != 0)
        def _():
            up.wait_recv()

        @pl.when(goes_up)
        def _():
            up.start()

        @pl.when(goes_down)
        def _():
            down.start()

    def across(buffer, i):
        return remote(buffer.at[core], buffer.at[core], cc_send.at[i], cc_recv.at[i], p, partner)

    @pl.loop(1, NC)
    def _(j):
        remote(rs, rows.at[core, 0], ra_send.at[0], ra_recv.at[lax.rem(chip + j, NC)], p, partner).wait_recv()

    across(rows, 0).start()

    @pl.loop(1, NC)
    def _(j):
        remote(hs, head.at[core, 0], ha_send.at[0], ha_recv.at[lax.rem(chip + j, NC)], p, partner).wait_recv()

    across(head, 1).start()
    across(head, 1).wait_recv()

    def block(i, j):
        return head[:, :, i, j].reshape(B, B)

    a = {(i, j): block(i, j) for i in range(PANELS) for j in range(PANELS)}
    halves = {}
    for k in range(PANELS):
        inverse = invert(a[k, k])
        fact[k, k] = inverse
        halves[k, k] = split(inverse)
        for j in range(k + 1, PANELS):
            fact[k, j] = a[k, j]
            halves[k, j] = split(a[k, j])
        for i in range(k + 1, PANELS):
            factor = dot3(split(a[i, k]), halves[k, k])
            fact[i, k] = factor
            halves[i, k] = split(factor)
            for j in range(k + 1, PANELS):
                a[i, j] = a[i, j] - dot3(halves[i, k], halves[k, j])

    is_panel = q < PANELS
    eye = (
        lax.broadcasted_iota(jnp.int32, (B, B), 0) == lax.broadcasted_iota(jnp.int32, (B, B), 1)
    ).astype(jnp.float32)
    y = []
    for i in range(PANELS):
        value = cols[i]
        for k in range(i):
            value = value - dot3(halves[i, k], y[k])
        upper[i] = value
        y.append(split(value))

    right = [None] * PANELS
    for i in reversed(range(PANELS)):
        value = jnp.where(is_panel, jnp.where(q == i, eye, 0.0), upper[i])
        for k in range(i + 1, PANELS):
            value = value - dot3(halves[i, k], right[k])
        right[i] = split(dot3(halves[i, i], split(value)))

    across(rows, 0).wait_recv()
    keep = jnp.where(is_panel, 0.0, 1.0)
    sign = jnp.where(is_panel, 1.0, -1.0)
    for b in range(2):
        total = jnp.zeros((B, B), jnp.float32)
        for k in range(PANELS):
            total = total + dot3(split(rows[:, :, k, b].reshape(B, B)), right[k])
        out_ref[b] = keep * x_ref[b] + sign * total

    @pl.when((p < PANELS) & is_panel)
    def _():
        out_ref[0] = fact[lax.rem(p, PANELS), lax.rem(q, PANELS)]

    @pl.when((p < PANELS) & (q >= PANELS))
    def _():
        out_ref[0] = upper[lax.rem(p, PANELS)]

    @pl.when(q < PANELS)
    def _():
        @pl.loop(1, NQ)
        def _(j):
            scatter(j).wait_send()

    @pl.when(p < PANELS)
    def _():
        @pl.loop(1, NP)
        def _(j):
            head_along(j).wait_send()

    @pl.loop(1, NC)
    def _(j):
        gather(rs, rows, ra_send, ra_recv, j).wait_send()
        gather(hs, head, ha_send, ha_recv, j).wait_send()

    @pl.loop(0, PANELS * CHUNKS)
    def _(i):
        _, up, down, goes_up, goes_down = chunk(i)

        @pl.when(goes_up)
        def _():
            up.wait_send()

        @pl.when(goes_down)
        def _():
            down.wait_send()

    across(rows, 0).wait_send()
    across(head, 1).wait_send()


def body(matrix):
    shape = matrix.shape
    f32 = jnp.float32
    dma = pltpu.SemaphoreType.DMA
    out = pl.pallas_call(
        kernel,
        out_shape=jax.ShapeDtypeStruct((2, B, B), f32),
        in_specs=[pl.BlockSpec(memory_space=pltpu.VMEM)],
        out_specs=pl.BlockSpec(memory_space=pltpu.VMEM),
        scratch_shapes=[
            pltpu.VMEM((PANELS, 2, S, B), f32),
            pltpu.VMEM((2, NC, PANELS, 2, S, B), f32),
            pltpu.VMEM((PANELS, PANELS, S, B), f32),
            pltpu.VMEM((2, NC, PANELS, PANELS, S, B), f32),
            pltpu.VMEM((PANELS, B, B), f32),
            pltpu.VMEM((PANELS, PANELS, B, B), f32),
            pltpu.VMEM((PANELS, B, B), f32),
            dma((NQ,)),
            dma((PANELS,)),
            dma((NC,)),
            dma((NC,)),
            dma((NP,)),
            dma((PANELS,)),
            dma((NC,)),
            dma((NC,)),
            dma((PANELS * CHUNKS,)),
            dma((PANELS * CHUNKS,)),
            dma((PANELS * CHUNKS,)),
            dma((2,)),
            dma((2,)),
        ],
        compiler_params=pltpu.CompilerParams(
            collective_id=0, has_side_effects=True, vmem_limit_bytes=48 * 1024 * 1024
        ),
    )(matrix.reshape(2, B, B))
    return out.reshape(shape)


def solution(mesh):
    spec = P(None, "prow", None, "pcol", None)
    return jax.shard_map(body, mesh=mesh, in_specs=(spec,), out_specs=spec, check_vma=False)
```

time: 846 us -> 192 us (0.23)
  the two profiles are of different devices: /device:TPU:1 before, /device:TPU:289 now
where the time goes in v1:
time: 192 us
  Pallas kernels  189 us (98%)
  local copies, waits for them, and re-layouts  2.41 us (1%)
    pallas_call x1, Pallas kernels, body(): pl.pallas_call(kernel, out_shape=jax.ShapeDtypeStruct((2, B, B), f32), in...  189 us

profile of v1, /device:TPU:289, one launch (start us, length us, event | category | flops | bytes accessed | tf_op | source)
XLA Modules:
  0.0 191.8 jit_solution(9433245190302747867)
XLA Ops:
  0.0 1.1 copy.5
  1.1 189.4 %shard_map.17 = f32[2,256,256]{2,1,0:T(8,128)S(1)} custom-call(f32[2,256,256]{2,1,0:T(8,128)S(1)} %bitcast.5), custom_call_target="tpu_custom_call" | custom-call | tf_op jit(solution)/shard_map/pallas_call | solution.py:285
  190.5 1.3 copy.2

commit v2 on v1

v2 whole, which is shorter than its diff:
```python
import functools

import jax
import jax.numpy as jnp
from jax import lax
from jax.experimental import pallas as pl
from jax.experimental.pallas import tpu as pltpu
from jax.sharding import PartitionSpec as P

B = 256
PANELS = 3
NP = 16
NQ = 32
NC = NQ // 2
S = B // NC
CHUNKS = 8
CR = B // CHUNKS
MESH = pl.DeviceIdType.MESH
STEPS0 = (2, 1, -1, -2)
STEPS1 = (4, 1, -1, -2, -4)


def split(value):
    high = value.astype(jnp.bfloat16)
    return high, (value - high.astype(jnp.float32)).astype(jnp.bfloat16)


def dot3(left, right):
    dot = functools.partial(jnp.dot, preferred_element_type=jnp.float32)
    return dot(left[0], right[0]) + (dot(left[0], right[1]) + dot(left[1], right[0]))


def invert(block):
    row = lax.broadcasted_iota(jnp.int32, (B, B), 0)
    col = lax.broadcasted_iota(jnp.int32, (B, B), 1)
    eye = row == col
    diagonal = jnp.where(eye, block, 0.0)
    down = 1.0 / jnp.sum(diagonal, axis=1, keepdims=True)
    across = 1.0 / jnp.sum(diagonal, axis=0, keepdims=True)
    first = jnp.where(eye, 2.0 * down, 0.0) - down * block * across
    parts = split(first)
    inner = dot3(split(block), parts)
    return 2.0 * first - dot3(parts, split(inner))


def wrap(p):
    return lax.rem(p + 2 * NP, NP)


def col_edge(step, away):
    if step == 2:
        return (away == 0) | (away == 2) | (away == 4) | (away == 6)
    if step == -2:
        return (away == 0) | (away == 14) | (away == 12)
    if step == -1:
        return (away == 2) | (away == 4) | (away == 6) | (away == 8)
    return (away == 8) | (away == 14) | (away == 12) | (away == 10)


def edge0(step, p):
    found = col_edge(step, wrap(p))
    for k in range(1, PANELS):
        found = found | col_edge(step, wrap(p - k))
    return found


def edge1(step, p):
    near = lax.rem(p, 4)
    if step == 4:
        return (near < PANELS) & (p < 8)
    if step == -4:
        return p < PANELS
    return near < PANELS


def kernel(
    x_ref,
    out_ref,
    rs,
    rows,
    hs,
    head,
    cols,
    fact,
    upper,
    ready0,
    ready1,
    sc_send,
    sc_recv,
    ra_send,
    ra_recv,
    hz_send,
    hz_recv,
    ha_send,
    ha_recv,
    z_send,
    z_recv,
    own_send,
    own_recv,
    zc_send,
    zc_recv,
    cc_send,
    cc_recv,
):
    p = lax.axis_index("prow")
    q = lax.axis_index("pcol")
    core = lax.rem(q, 2)
    chip = q // 2
    partner = q + 1 - 2 * core
    is_zero = core == 0
    is_one = core == 1
    is_root = p < PANELS
    scatters = (q == 0) | (q == 2)

    def remote(src, dst, send, recv, row, col):
        return pltpu.make_async_remote_copy(
            src_ref=src, dst_ref=dst, send_sem=send, recv_sem=recv, device_id=(row, col), device_id_type=MESH
        )

    def signal(sem, row, col):
        pl.semaphore_signal(sem, inc=1, device_id=(row, col), device_id_type=MESH)

    def count(flag):
        return flag.astype(jnp.int32)

    barrier = pltpu.get_barrier_semaphore()

    def greet(steps, edge):
        for s in steps:
            child, parent = wrap(p + s), wrap(p - s)

            @pl.when(edge(s, p) & (p < child))
            def _():
                signal(barrier, child, q)

            @pl.when(edge(s, parent) & (parent > p))
            def _():
                signal(barrier, parent, q)

    def greetings(steps, edge):
        total = 0
        for s in steps:
            child, parent = wrap(p + s), wrap(p - s)
            total = total + count(edge(s, parent) & (parent < p)) + count(edge(s, p) & (child < p))
        return total

    def answer(steps, edge, ready):
        for i, s in enumerate(steps):
            parent = wrap(p - s)

            @pl.when(edge(s, parent) & (parent < p))
            def _():
                signal(ready.at[i], parent, q)

    def await_ready(steps, edge, ready, s):
        @pl.when(edge(s, p) & (p < wrap(p + s)))
        def _():
            pl.semaphore_wait(ready.at[steps.index(s)], 1)

    @pl.when(is_zero)
    def _():
        greet(STEPS0, edge0)

        @pl.when(scatters)
        def _():
            @pl.loop(0, NC)
            def _(j):
                signal(barrier, p, 2 * j + 1)

        @pl.when(jnp.logical_not(scatters))
        def _():
            signal(barrier, p, partner)

        pl.semaphore_wait(barrier, greetings(STEPS0, edge0) + 1 + (NC - 1) * count(scatters))
        answer(STEPS0, edge0, ready0)

    @pl.when(is_one)
    def _():
        greet(STEPS1, edge1)

        @pl.loop(1, NC)
        def _(j):
            signal(barrier, p, lax.rem(q + 2 * j, NQ))

        for t in (0, 2):

            @pl.when(partner != t)
            def _():
                signal(barrier, p, t)

        signal(barrier, p, partner)
        others = NC - 1 + 3 - count((partner == 0) | (partner == 2))
        pl.semaphore_wait(barrier, greetings(STEPS1, edge1) + others)
        answer(STEPS1, edge1, ready1)

    def scatter(t):
        piece = x_ref.at[:, pl.ds(pl.multiple_of(t * S, S), S)]
        return remote(piece, rs.at[lax.rem(q, PANELS)], sc_send.at[t], sc_recv.at[lax.rem(q, PANELS)], p, 2 * t + 1)

    def each_scatter(act):
        @pl.when(q < PANELS)
        def _():
            @pl.loop(0, NC)
            def _(t):
                @pl.when(2 * t + 1 != q)
                def _():
                    act(scatter(t))

    def own():
        return remote(x_ref.at[0], cols.at[1, lax.rem(p, PANELS)], own_send, own_recv, p, partner)

    @pl.when(is_one & is_root)
    def _():
        own().start()

    each_scatter(lambda copy: copy.start())

    def col_piece(i):
        return pl.ds(pl.multiple_of(i * CR, CR), CR)

    def col_copy(k, i, step):
        piece = cols.at[:, k, col_piece(i)]
        n = STEPS0.index(step)
        return remote(piece, piece, z_send.at[n, k * CHUNKS + i], z_recv.at[k * CHUNKS + i], wrap(p + step), q)

    def to_one(k, i):
        piece = cols.at[1, k, col_piece(i)]
        return remote(piece, piece, zc_send.at[k], zc_recv.at[k], p, partner)

    @pl.when(is_zero)
    def _():
        mine = lax.rem(p, PANELS)

        @pl.when(is_root)
        def _():
            cols[0, mine] = x_ref[0]
            own().wait_recv()

        for s in (2, 1, -1, -2):
            await_ready(STEPS0, edge0, ready0, s)
            if s in (2, -2):

                @pl.when(is_root)
                def _():
                    @pl.loop(0, CHUNKS)
                    def _(i):
                        col_copy(mine, i, s).start()

        @pl.loop(0, CHUNKS)
        def _(i):
            for k in reversed(range(PANELS)):
                away = wrap(p - k)

                @pl.when((lax.rem(away, 2) == 0) & (away != 0))
                def _():
                    col_copy(k, i, 2).wait_recv()
                    for s in STEPS0:

                        @pl.when(col_edge(s, away))
                        def _():
                            col_copy(k, i, s).start()

                    to_one(k, i).start()

        @pl.loop(0, CHUNKS)
        def _(i):
            for k in range(PANELS):

                @pl.when(lax.rem(wrap(p - k), 2) == 1)
                def _():
                    col_copy(k, i, 2).wait_recv()
                    to_one(k, i).start()

    def gather(src, dst, send, recv, j):
        return remote(src, dst.at[chip], send.at[j], recv.at[chip], p, lax.rem(q + 2 * j, NQ))

    def across(buffer, i, j):
        return remote(buffer.at[j], buffer.at[j], cc_send.at[i], cc_recv.at[i], p, partner)

    def whole(buffer, i):
        return remote(buffer, buffer, cc_send.at[i], cc_recv.at[i], p, partner)

    near = lax.rem(p, 4)
    mine4 = lax.rem(near, PANELS)
    anchor = near < PANELS

    def along(step):
        n = STEPS1.index(step)
        return remote(hs.at[mine4], hs.at[mine4], hz_send.at[n], hz_recv.at[mine4], wrap(p + step), q)

    def hand_over(src, buffer, recv, i):
        across(buffer, i, chip).start()

        @pl.loop(1, NC)
        def _(j):
            c = lax.rem(chip + j, NC)
            remote(src, buffer.at[c], ra_send.at[0], recv.at[c], p, partner).wait_recv()
            across(buffer, i, c).start()

    @pl.when(is_one)
    def _():
        @pl.when(q == 1)
        def _():
            rs[1] = x_ref[:, 0:S]

        for k in range(PANELS):

            @pl.when(q != k)
            def _():
                remote(x_ref.at[:, pl.ds(0, S)], rs.at[k], sc_send.at[0], sc_recv.at[k], p, partner).wait_recv()

        @pl.when(is_root)
        def _():
            hs[mine4] = rs[:, 0]

        @pl.when(anchor & jnp.logical_not(is_root))
        def _():
            along(4).wait_recv()

        for s in STEPS1:
            await_ready(STEPS1, edge1, ready1, s)

            @pl.when(edge1(s, p))
            def _():
                along(s).start()

        rows[chip] = rs[...]

        @pl.loop(1, NC)
        def _(j):
            gather(rs, rows, ra_send, ra_recv, j).start()

        for k in range(PANELS):

            @pl.when(near != k)
            def _():
                remote(hs.at[k], hs.at[k], hz_send.at[0], hz_recv.at[k], p, partner).wait_recv()

        head[chip] = hs[...]

        @pl.loop(1, NC)
        def _(j):
            gather(hs, head, ha_send, ha_recv, j).start()

        @pl.when(is_root)
        def _():
            cols[1, lax.rem(p, PANELS)] = x_ref[0]

        hand_over(rs, rows, ra_recv, 0)
        hand_over(hs, head, ha_recv, 1)

    @pl.when(is_zero)
    def _():
        whole(head, 1).wait_recv()

    def block(i, j):
        return head[:, i, j].reshape(B, B)

    a = {(i, j): block(i, j) for i in range(PANELS) for j in range(PANELS)}
    halves = {}
    for k in range(PANELS):
        inverse = invert(a[k, k])
        fact[k, k] = inverse
        halves[k, k] = split(inverse)
        for j in range(k + 1, PANELS):
            fact[k, j] = a[k, j]
            halves[k, j] = split(a[k, j])
        for i in range(k + 1, PANELS):
            factor = dot3(split(a[i, k]), halves[k, k])
            fact[i, k] = factor
            halves[i, k] = split(factor)
            for j in range(k + 1, PANELS):
                a[i, j] = a[i, j] - dot3(halves[i, k], halves[k, j])

    @pl.when(is_one)
    def _():
        for k in range(PANELS):

            @pl.when(p != k)
            def _():
                remote(cols.at[1, k], cols.at[1, k], zc_send.at[k], zc_recv.at[k], p, partner).wait_recv()

    is_panel = q < PANELS
    eye = (
        lax.broadcasted_iota(jnp.int32, (B, B), 0) == lax.broadcasted_iota(jnp.int32, (B, B), 1)
    ).astype(jnp.float32)
    y = []
    for i in range(PANELS):
        value = cols[core, i]
        for k in range(i):
            value = value - dot3(halves[i, k], y[k])
        upper[i] = value
        y.append(split(value))

    right = [None] * PANELS
    for i in reversed(range(PANELS)):
        value = jnp.where(is_panel, jnp.where(q == i, eye, 0.0), upper[i])
        for k in range(i + 1, PANELS):
            value = value - dot3(halves[i, k], right[k])
        right[i] = split(dot3(halves[i, i], split(value)))

    @pl.when(is_zero)
    def _():
        whole(rows, 0).wait_recv()

    keep = jnp.where(is_panel, 0.0, 1.0)
    sign = jnp.where(is_panel, 1.0, -1.0)
    for b in range(2):
        total = jnp.zeros((B, B), jnp.float32)
        for k in range(PANELS):
            total = total + dot3(split(rows[:, k, b].reshape(B, B)), right[k])
        out_ref[b] = keep * x_ref[b] + sign * total

    @pl.when(is_root & is_panel)
    def _():
        out_ref[0] = fact[lax.rem(p, PANELS), lax.rem(q, PANELS)]

    @pl.when(is_root & (q >= PANELS))
    def _():
        out_ref[0] = upper[lax.rem(p, PANELS)]

    each_scatter(lambda copy: copy.wait_send())

    @pl.when(is_zero)
    def _():
        for k in range(PANELS):
            away = wrap(p - k)
            for s in STEPS0:

                @pl.when(col_edge(s, away))
                def _():
                    @pl.loop(0, CHUNKS)
                    def _(i):
                        col_copy(k, i, s).wait_send()

            @pl.when(away != 0)
            def _():
                remote(cols.at[1, k], cols.at[1, k], zc_send.at[k], zc_recv.at[k], p, partner).wait_send()

    @pl.when(is_one)
    def _():
        @pl.when(is_root)
        def _():
            own().wait_send()

        for s in STEPS1:

            @pl.when(edge1(s, p))
            def _():
                along(s).wait_send()

        @pl.loop(1, NC)
        def _(j):
            gather(rs, rows, ra_send, ra_recv, j).wait_send()
            gather(hs, head, ha_send, ha_recv, j).wait_send()

        whole(rows, 0).wait_send()
        whole(head, 1).wait_send()


def body(matrix):
    shape = matrix.shape
    f32 = jnp.float32
    dma = pltpu.SemaphoreType.DMA
    out = pl.pallas_call(
        kernel,
        out_shape=jax.ShapeDtypeStruct((2, B, B), f32),
        in_specs=[pl.BlockSpec(memory_space=pltpu.VMEM)],
        out_specs=pl.BlockSpec(memory_space=pltpu.VMEM),
        scratch_shapes=[
            pltpu.VMEM((PANELS, 2, S, B), f32),
            pltpu.VMEM((NC, PANELS, 2, S, B), f32),
            pltpu.VMEM((PANELS, PANELS, S, B), f32),
            pltpu.VMEM((NC, PANELS, PANELS, S, B), f32),
            pltpu.VMEM((2, PANELS, B, B), f32),
            pltpu.VMEM((PANELS, PANELS, B, B), f32),
            pltpu.VMEM((PANELS, B, B), f32),
            pltpu.SemaphoreType.REGULAR((len(STEPS0),)),
            pltpu.SemaphoreType.REGULAR((len(STEPS1),)),
            dma((NC,)),
            dma((PANELS,)),
            dma((NC,)),
            dma((NC,)),
            dma((len(STEPS1),)),
            dma((PANELS,)),
            dma((NC,)),
            dma((NC,)),
            dma((len(STEPS0), PANELS * CHUNKS)),
            dma((PANELS * CHUNKS,)),
            dma,
            dma,
            dma((PANELS,)),
            dma((PANELS,)),
            dma((2,)),
            dma((2,)),
        ],
        compiler_params=pltpu.CompilerParams(
            collective_id=0, has_side_effects=True, vmem_limit_bytes=48 * 1024 * 1024
        ),
    )(matrix.reshape(2, B, B))
    return out.reshape(shape)


def solution(mesh):
    spec = P(None, "prow", None, "pcol", None)
    return jax.shard_map(body, mesh=mesh, in_specs=(spec,), out_specs=spec, check_vma=False)
```

time: 192 us -> 66.5 us (0.35)
  the two profiles are of different devices: /device:TPU:289 before, /device:TPU:352 now
where the time goes in v2:
time: 66.5 us; the launch traced here: 66.4 us
  Pallas kernels  63.9 us (96%)
  local copies, waits for them, and re-layouts  2.41 us (4%)
    pallas_call x1, Pallas kernels, body(): pl.pallas_call(kernel, out_shape=jax.ShapeDtypeStruct((2, B, B), f32), in...  63.9 us
    reshape x1, local copies, waits for them, and re-layouts, body(): return out.reshape(shape)  1.33 us

profile of v2, /device:TPU:352, one launch (start us, length us, event | category | flops | bytes accessed | tf_op | source)
XLA Modules:
  0.0 66.4 jit_solution(10520100442980554384)
XLA Ops:
  0.0 1.1 %copy.5 = f32[2,1,256,1,256]{4,2,3,1,0:T(8,128)S(1)} copy(f32[2,1,256,1,256]{4,3,2,1,0:T(1,128)} %param.1) | data formatting | bytes 1048576
  1.1 63.9 %shard_map.17 = f32[2,256,256]{2,1,0:T(8,128)S(1)} custom-call(f32[2,256,256]{2,1,0:T(8,128)S(1)} %bitcast.5), custom_call_target="tpu_custom_call" | custom-call | tf_op jit(solution)/shard_map/pallas_call | solution.py:465
  65.0 1.3 %copy.2 = f32[2,1,256,1,256]{4,3,2,1,0:T(1,128)} copy(f32[2,1,256,1,256]{4,2,0,3,1:T(8,128)S(1)} %bitcast.4) | data formatting | bytes 1048576 | tf_op jit(solution)/shard_map/reshape | solution.py:501

commit v3 on v2

v3 whole, which is shorter than its diff:
```python
import functools

import jax
import jax.numpy as jnp
from jax import lax
from jax.experimental import pallas as pl
from jax.experimental.pallas import tpu as pltpu
from jax.sharding import PartitionSpec as P

B = 256
PANELS = 3
NP = 16
NQ = 32
NC = NQ // 2
S = B // NC // 2
SIDE = 4
CHUNKS = 8
CR = 2 * B // CHUNKS
WINDOW = 3
LAG = 3
MESH = pl.DeviceIdType.MESH
STEPS0 = (2, 1, -1, -2)
STEPS1 = (4, 1, -1, -2, -4)


def split(value):
    high = value.astype(jnp.bfloat16)
    return high, (value - high.astype(jnp.float32)).astype(jnp.bfloat16)


def dot3(left, right):
    dot = functools.partial(jnp.dot, preferred_element_type=jnp.float32)
    return dot(left[0], right[0]) + (dot(left[0], right[1]) + dot(left[1], right[0]))


def invert(block):
    row = lax.broadcasted_iota(jnp.int32, (B, B), 0)
    col = lax.broadcasted_iota(jnp.int32, (B, B), 1)
    eye = row == col
    diagonal = jnp.where(eye, block, 0.0)
    down = 1.0 / jnp.sum(diagonal, axis=1, keepdims=True)
    across = 1.0 / jnp.sum(diagonal, axis=0, keepdims=True)
    first = jnp.where(eye, 2.0 * down, 0.0) - down * block * across
    parts = split(first)
    inner = dot3(split(block), parts)
    return 2.0 * first - dot3(parts, split(inner))


def wrap(p):
    return lax.rem(p + 2 * NP, NP)


def among(value, choices):
    found = value == choices[0]
    for c in choices[1:]:
        found = found | (value == c)
    return found


ON = (
    {2: (0, 2, 4, 6, 8), -2: (0, 14), -1: (2, 4, 6, 8, 10), 1: (10, 12, 14)},
    {2: (0, 2, 4), -2: (0, 14, 12, 10), -1: (2, 4, 6, 8), 1: (8, 10, 12, 14)},
)


def edge0(step, p):
    places = sorted(set(ON[0][step]) | set(ON[1][step]))
    found = among(wrap(p), places)
    for k in range(1, PANELS):
        found = found | among(wrap(p - k), places)
    return found


def edge1(step, p):
    near = lax.rem(p, 4)
    if step == 4:
        return (near < PANELS) & (p < 8)
    if step == -4:
        return p < PANELS
    return near < PANELS


def kernel(
    x_ref,
    out_ref,
    rs,
    rows,
    hs,
    head,
    cols,
    fact,
    upper,
    ready0,
    ready1,
    sc_send,
    sc_recv,
    ra_send,
    ra_recv,
    hz_send,
    hz_recv,
    ha_send,
    ha_recv,
    z_send,
    z_recv,
    own_send,
    own_recv,
    zc_send,
    zc_recv,
    cc_send,
    cc_recv,
):
    p = lax.axis_index("prow")
    q = lax.axis_index("pcol")
    core = lax.rem(q, 2)
    chip = q // 2
    chip_y, chip_x = chip // SIDE, lax.rem(chip, SIDE)
    partner = q + 1 - 2 * core
    is_zero = core == 0
    is_one = core == 1
    is_root = p < PANELS
    scatters = (q == 0) | (q == 2)
    flows = chip > 0

    def remote(src, dst, send, recv, row, col):
        return pltpu.make_async_remote_copy(
            src_ref=src, dst_ref=dst, send_sem=send, recv_sem=recv, device_id=(row, col), device_id_type=MESH
        )

    def signal(sem, row, col):
        pl.semaphore_signal(sem, inc=1, device_id=(row, col), device_id_type=MESH)

    def count(flag):
        return flag.astype(jnp.int32)

    barrier = pltpu.get_barrier_semaphore()

    def greet(steps, edge):
        for s in steps:
            child, parent = wrap(p + s), wrap(p - s)

            @pl.when(edge(s, p) & (p < child))
            def _():
                signal(barrier, child, q)

            @pl.when(edge(s, parent) & (parent > p))
            def _():
                signal(barrier, parent, q)

    def greetings(steps, edge, twice=()):
        total = 0
        for s in steps:
            child, parent = wrap(p + s), wrap(p - s)
            total = total + count(edge(s, parent) & (parent < p)) + (1 + (s in twice)) * count(edge(s, p) & (child < p))
        return total

    def answer(steps, edge, ready):
        for i, s in enumerate(steps):
            parent = wrap(p - s)

            @pl.when(edge(s, parent) & (parent < p))
            def _():
                signal(ready.at[i], parent, q)

    def await_ready(steps, edge, ready, s):
        @pl.when(edge(s, p) & (p < wrap(p + s)))
        def _():
            pl.semaphore_wait(ready.at[steps.index(s)], 1)

    @pl.when(is_zero)
    def _():
        @pl.when(flows)
        def _():
            greet(STEPS0, edge0)

        @pl.when(scatters)
        def _():
            @pl.loop(0, NC)
            def _(j):
                signal(barrier, p, 2 * j + 1)

        @pl.when(jnp.logical_not(scatters))
        def _():
            signal(barrier, p, partner)

        pl.semaphore_wait(barrier, greetings(STEPS0, edge0, (1, -1)) * count(flows) + 1 + (NC - 1) * count(scatters))

        @pl.when(flows)
        def _():
            answer(STEPS0, edge0, ready0)

    @pl.when(is_one)
    def _():
        greet(STEPS1, edge1)

        for s in (1, -1):
            parent = wrap(p - s)

            @pl.when(flows & edge0(s, parent) & (parent > p))
            def _():
                signal(barrier, parent, partner)

        for step in (1, -1):
            signal(barrier, p, 2 * (chip_y * SIDE + lax.rem(chip_x + step + SIDE, SIDE)) + 1)
            signal(barrier, p, 2 * (lax.rem(chip_y + step + SIDE, SIDE) * SIDE + chip_x) + 1)

        for t in range(PANELS):

            @pl.when((partner != t) & (q != t))
            def _():
                signal(barrier, p, t)

        @pl.when(q == 1)
        def _():
            @pl.loop(1, NC)
            def _(j):
                signal(barrier, p, 2 * j + 1)

        signal(barrier, p, partner)
        others = 4 + 4 - count((partner == 0) | (partner == 2)) + (NC - 2) * count(q == 1)
        pl.semaphore_wait(barrier, greetings(STEPS1, edge1) + others)
        answer(STEPS1, edge1, ready1)

    def scatter(t):
        return remote(x_ref.at[:, :, t], rs.at[lax.rem(q, PANELS)], sc_send.at[t], sc_recv.at[lax.rem(q, PANELS)], p, 2 * t + 1)

    def each_scatter(act):
        @pl.when(q < PANELS)
        def _():
            @pl.loop(0, NC)
            def _(t):
                @pl.when(2 * t + 1 != q)
                def _():
                    act(scatter(t))

    def own(half):
        piece = cols.at[1, lax.rem(p, PANELS), half]
        return remote(x_ref.at[0, half], piece, own_send.at[half], own_recv.at[half], p, partner)

    @pl.when(is_one & is_root & flows)
    def _():
        own(0).start()
        own(1).start()

    each_scatter(lambda copy: copy.start())

    def col_piece(k, i):
        half, j = i // 4, lax.rem(i, 4)
        return cols.at[j // 2, k, half, pl.ds(lax.rem(j, 2) * (CR // S), CR // S)]

    def col_copy(k, i, step):
        piece = col_piece(k, i)
        n = STEPS0.index(step)
        to = q + lax.rem(i, 4) // 2 if step in (1, -1) else q
        return remote(piece, piece, z_send.at[n, k * CHUNKS + i], z_recv.at[k * CHUNKS + i], wrap(p + step), to)

    def to_one(k, i):
        piece = col_piece(k, i)
        return remote(piece, piece, zc_send.at[k], zc_recv.at[k], p, partner)

    def pass_on(k, i, act):
        away = wrap(p - k)
        for half in range(2):

            @pl.when(i // 4 == half)
            def _():
                for s in STEPS0:

                    @pl.when(among(away, ON[half][s]))
                    def _():
                        act(col_copy(k, i, s))

    def in_turn(k, i):
        away = wrap(p - k)
        return lax.rem(i + 4 * count(away > 8), CHUNKS)

    @pl.when(is_zero & flows)
    def _():
        mine = lax.rem(p, PANELS)

        def start_own(n, step):
            first = 0 if step == 2 else 4

            @pl.when(is_root & (n < CHUNKS))
            def _():
                @pl.when(n >= WINDOW)
                def _():
                    col_copy(mine, lax.rem(n - WINDOW + first, CHUNKS), step).wait_send()

                col_copy(mine, lax.rem(n + first, CHUNKS), step).start()

        @pl.when(is_root)
        def _():
            cols[0, mine] = x_ref[0]

        await_ready(STEPS0, edge0, ready0, 2)

        @pl.loop(0, CHUNKS + LAG)
        def _(n):
            for half, turn in ((0, 2), (1, LAG + 2)):

                @pl.when(is_root & (n == turn))
                def _():
                    own(half).wait_recv()

            start_own(n, 2)

            @pl.when(n == LAG)
            def _():
                for s in (-2, -1, 1):
                    await_ready(STEPS0, edge0, ready0, s)

            @pl.when(n >= LAG)
            def _():
                i = n - LAG
                start_own(i, -2)
                for k in reversed(range(PANELS)):
                    away = wrap(p - k)

                    @pl.when((lax.rem(away, 2) == 0) & (away != 0))
                    def _():
                        t = in_turn(k, i)
                        col_copy(k, t, 2).wait_recv()
                        pass_on(k, t, lambda copy: copy.start())

                        @pl.when(lax.rem(t, 4) >= 2)
                        def _():
                            to_one(k, t).start()

        @pl.when(is_root)
        def _():
            @pl.loop(CHUNKS - WINDOW, CHUNKS)
            def _(n):
                col_copy(mine, n, 2).wait_send()
                col_copy(mine, lax.rem(n + 4, CHUNKS), -2).wait_send()

    def await_fills():
        @pl.when(flows)
        def _():
            for k in range(PANELS):

                @pl.when(lax.rem(wrap(p - k), 2) == 1)
                def _():
                    @pl.loop(0, CHUNKS // 2)
                    def _(i):
                        col_copy(k, (i // 2) * 4 + core * 2 + lax.rem(i, 2), 2).wait_recv()

                @pl.when(is_one & (p != k) & (lax.rem(wrap(p - k), 2) == 0))
                def _():
                    remote(cols.at[1, k], cols.at[1, k], zc_send.at[k], zc_recv.at[k], p, partner).wait_recv()

    @pl.when(jnp.logical_not(flows))
    def _():
        cols[...] = jnp.zeros_like(cols)

    def across(buffer, n, half, c):
        piece = buffer.at[half, c]
        return remote(piece, piece, cc_send.at[n], cc_recv.at[n], p, partner)

    def whole(buffer, n):
        return remote(buffer, buffer, cc_send.at[n], cc_recv.at[n], p, partner)

    class Ring:
        def __init__(self, buffer, send, recv, n):
            self.buffer, self.send, self.recv, self.n = buffer, send, recv, n

        def line(self, stage, half, t, step):
            if stage == half:
                x = lax.rem(chip_x + step + SIDE, SIDE)
                return (chip_y if stage == 0 else t) * SIDE + x
            y = lax.rem(chip_y + step + SIDE, SIDE)
            return y * SIDE + (chip_x if stage == 0 else t)

        def neighbour(self, stage, half, step):
            if stage == half:
                return 2 * (chip_y * SIDE + lax.rem(chip_x + step + SIDE, SIDE)) + 1
            return 2 * (lax.rem(chip_y + step + SIDE, SIDE) * SIDE + chip_x) + 1

        def copy(self, stage, half, t, kind):
            step = 1 if kind in (0, 2) else -1
            piece = self.buffer.at[half, self.line(stage, half, t, 0 if kind < 2 else -step)]
            if kind >= 2:
                piece = piece.at[:, :, :, pl.ds((kind - 2) * (B // 2), B // 2)]
            i = (stage * SIDE + t) * 2 + half
            return remote(piece, piece, self.send.at[kind, i], self.recv.at[kind, i], p, self.neighbour(stage, half, step))

        def each(self, stage, act):
            if stage == 0:
                for half in range(2):
                    act(half, 0)
                return

            @pl.loop(0, SIDE)
            def _(t):
                for half in range(2):
                    act(half, t)

        def push(self, stage, half, t, step):
            if stage == 1:
                across(self.buffer, self.n, half, self.line(stage, half, t, step)).start()

        def begin(self, stage):
            def act(half, t):
                self.copy(stage, half, t, 0).start()
                self.copy(stage, half, t, 1).start()
                self.push(stage, half, t, 0)

            self.each(stage, act)

        def middle(self, stage):
            def act(half, t):
                for kind in range(2):
                    self.copy(stage, half, t, kind).wait_recv()
                    self.copy(stage, half, t, 2 + kind).start()
                    self.push(stage, half, t, -1 if kind == 0 else 1)

            self.each(stage, act)

        def end(self, stage):
            def act(half, t):
                for kind in (2, 3):
                    self.copy(stage, half, t, kind).wait_recv()
                self.push(stage, half, t, 2)

            self.each(stage, act)

        def sent(self):
            for stage in range(2):

                def act(half, t):
                    for kind in range(4):
                        self.copy(stage, half, t, kind).wait_send()

                self.each(stage, act)

    near = lax.rem(p, 4)
    mine4 = lax.rem(near, PANELS)
    anchor = near < PANELS

    def along(step):
        n = STEPS1.index(step)
        return remote(hs.at[mine4], hs.at[mine4], hz_send.at[n], hz_recv.at[mine4], wrap(p + step), q)

    row_ring = Ring(rows, ra_send, ra_recv, 0)
    head_ring = Ring(head, ha_send, ha_recv, 1)

    @pl.when(is_one)
    def _():
        @pl.when(q == 1)
        def _():
            rs[1] = x_ref[:, :, 0]

        for k in range(PANELS):

            @pl.when(q != k)
            def _():
                remote(x_ref.at[:, :, 0], rs.at[k], sc_send.at[0], sc_recv.at[k], p, partner).wait_recv()

        @pl.when(is_root)
        def _():
            hs[mine4] = rs[:, 0]

        @pl.when(anchor & jnp.logical_not(is_root))
        def _():
            along(4).wait_recv()

        for s in STEPS1:
            await_ready(STEPS1, edge1, ready1, s)

            @pl.when(edge1(s, p))
            def _():
                along(s).start()

        for half in range(2):
            rows[half, chip] = rs[:, :, half]
        row_ring.begin(0)
        row_ring.middle(0)

        for k in range(PANELS):

            @pl.when(near != k)
            def _():
                remote(hs.at[k], hs.at[k], hz_send.at[0], hz_recv.at[k], p, partner).wait_recv()

        for half in range(2):
            head[half, chip] = hs[:, :, half]
        head_ring.begin(0)
        row_ring.end(0)
        row_ring.begin(1)
        head_ring.middle(0)
        row_ring.middle(1)
        head_ring.end(0)
        head_ring.begin(1)

        @pl.when(is_root & flows)
        def _():
            cols[1, lax.rem(p, PANELS)] = x_ref[0]

        row_ring.end(1)
        head_ring.middle(1)
        head_ring.end(1)

    @pl.when(is_zero)
    def _():
        whole(head, 1).wait_recv()

    def block(i, j):
        return head[:, :, i, j].reshape(B, B)

    a = {(i, j): block(i, j) for i in range(PANELS) for j in range(PANELS)}
    halves = {}
    for k in range(PANELS):
        inverse = invert(a[k, k])
        fact[k, k] = inverse
        halves[k, k] = split(inverse)
        for j in range(k + 1, PANELS):
            fact[k, j] = a[k, j]
            halves[k, j] = split(a[k, j])
        for i in range(k + 1, PANELS):
            factor = dot3(split(a[i, k]), halves[k, k])
            fact[i, k] = factor
            halves[i, k] = split(factor)
            for j in range(k + 1, PANELS):
                a[i, j] = a[i, j] - dot3(halves[i, k], halves[k, j])

    await_fills()
    is_panel = q < PANELS
    eye = (
        lax.broadcasted_iota(jnp.int32, (B, B), 0) == lax.broadcasted_iota(jnp.int32, (B, B), 1)
    ).astype(jnp.float32)
    y = []
    for i in range(PANELS):
        value = cols[core, i].reshape(B, B)
        for k in range(i):
            value = value - dot3(halves[i, k], y[k])
        upper[i] = value
        y.append(split(value))

    right = [None] * PANELS
    for i in reversed(range(PANELS)):
        value = jnp.where(is_panel, jnp.where(q == i, eye, 0.0), upper[i])
        for k in range(i + 1, PANELS):
            value = value - dot3(halves[i, k], right[k])
        right[i] = split(dot3(halves[i, i], split(value)))

    @pl.when(is_zero)
    def _():
        whole(rows, 0).wait_recv()

    keep = jnp.where(is_panel, 0.0, 1.0)
    sign = jnp.where(is_panel, 1.0, -1.0)
    for b in range(2):
        total = jnp.zeros((B, B), jnp.float32)
        for k in range(PANELS):
            total = total + dot3(split(rows[:, :, k, b].reshape(B, B)), right[k])
        out_ref[b] = keep * x_ref[b].reshape(B, B) + sign * total

    @pl.when(is_root & is_panel)
    def _():
        out_ref[0] = fact[lax.rem(p, PANELS), lax.rem(q, PANELS)]

    @pl.when(is_root & (q >= PANELS))
    def _():
        out_ref[0] = upper[lax.rem(p, PANELS)]

    each_scatter(lambda copy: copy.wait_send())

    @pl.when(is_zero & flows)
    def _():
        @pl.loop(0, CHUNKS)
        def _(i):
            for k in range(PANELS):

                @pl.when(p != k)
                def _():
                    pass_on(k, i, lambda copy: copy.wait_send())

        for k in range(PANELS):

            @pl.when((p != k) & (lax.rem(wrap(p - k), 2) == 0))
            def _():
                remote(cols.at[1, k], cols.at[1, k], zc_send.at[k], zc_recv.at[k], p, partner).wait_send()

    @pl.when(is_one)
    def _():
        @pl.when(is_root & flows)
        def _():
            own(0).wait_send()
            own(1).wait_send()

        for s in STEPS1:

            @pl.when(edge1(s, p))
            def _():
                along(s).wait_send()

        row_ring.sent()
        head_ring.sent()
        whole(rows, 0).wait_send()
        whole(head, 1).wait_send()


def body(matrix):
    shape = matrix.shape
    f32 = jnp.float32
    dma = pltpu.SemaphoreType.DMA
    out = pl.pallas_call(
        kernel,
        out_shape=jax.ShapeDtypeStruct((2, B, B), f32),
        in_specs=[pl.BlockSpec(memory_space=pltpu.VMEM)],
        out_specs=pl.BlockSpec(memory_space=pltpu.VMEM),
        scratch_shapes=[
            pltpu.VMEM((PANELS, 2, 2, S, B), f32),
            pltpu.VMEM((2, NC, PANELS, 2, S, B), f32),
            pltpu.VMEM((PANELS, PANELS, 2, S, B), f32),
            pltpu.VMEM((2, NC, PANELS, PANELS, S, B), f32),
            pltpu.VMEM((2, PANELS, 2, NC, S, B), f32),
            pltpu.VMEM((PANELS, PANELS, B, B), f32),
            pltpu.VMEM((PANELS, B, B), f32),
            pltpu.SemaphoreType.REGULAR((len(STEPS0),)),
            pltpu.SemaphoreType.REGULAR((len(STEPS1),)),
            dma((NC,)),
            dma((PANELS,)),
            dma((4, 4 * SIDE)),
            dma((4, 4 * SIDE)),
            dma((len(STEPS1),)),
            dma((PANELS,)),
            dma((4, 4 * SIDE)),
            dma((4, 4 * SIDE)),
            dma((len(STEPS0), PANELS * CHUNKS)),
            dma((PANELS * CHUNKS,)),
            dma((2,)),
            dma((2,)),
            dma((PANELS,)),
            dma((PANELS,)),
            dma((2,)),
            dma((2,)),
        ],
        compiler_params=pltpu.CompilerParams(
            collective_id=0, has_side_effects=True, vmem_limit_bytes=48 * 1024 * 1024
        ),
    )(matrix.reshape(2, 2, NC, S, B))
    return out.reshape(shape)


def solution(mesh):
    spec = P(None, "prow", None, "pcol", None)
    return jax.shard_map(body, mesh=mesh, in_specs=(spec,), out_specs=spec, check_vma=False)
```

time: 66.5 us -> 54.8 us (0.82)
  the two profiles are of different devices: /device:TPU:352 before, /device:TPU:227 now
where the time goes in v3:
time: 54.8 us; the launch traced here: 54.7 us
  Pallas kernels  52.3 us (95%)
  local copies, waits for them, and re-layouts  2.41 us (4%)
    pallas_call x1, Pallas kernels, body(): pl.pallas_call(kernel, out_shape=jax.ShapeDtypeStruct((2, B, B), f32), in...  52.3 us
    reshape x1, local copies, waits for them, and re-layouts, body(): return out.reshape(shape)  1.33 us

profile of v3, /device:TPU:227, one launch (start us, length us, event | category | flops | bytes accessed | tf_op | source)
XLA Modules:
  0.0 54.7 jit_solution(10265021746320231981)
XLA Ops:
  0.0 1.1 %copy.3 = f32[2,1,256,1,256]{4,2,3,1,0:T(8,128)S(1)} copy(f32[2,1,256,1,256]{4,3,2,1,0:T(1,128)} %param.1) | data formatting | bytes 1048576
  1.1 52.3 %shard_map.17 = f32[2,256,256]{2,1,0:T(8,128)S(1)} custom-call(f32[2,2,16,8,256]{4,3,2,1,0:T(8,128)S(1)} %bitcast.3), custom_call_target="tpu_custom_call" | custom-call | tf_op jit(solution)/shard_map/pallas_call | solution.py:606
  53.4 1.3 %copy.2 = f32[2,1,256,1,256]{4,3,2,1,0:T(1,128)} copy(f32[2,1,256,1,256]{4,2,0,3,1:T(8,128)S(1)} %bitcast.2) | data formatting | bytes 1048576 | tf_op jit(solution)/shard_map/reshape | solution.py:642

commit v4 on v3

--- a/solution.py
+++ b/solution.py
@@ -16,7 +16,7 @@
 SIDE = 4
 CHUNKS = 8
 CR = 2 * B // CHUNKS
-WINDOW = 3
+WINDOW = 2
 LAG = 3
 MESH = pl.DeviceIdType.MESH
 STEPS0 = (2, 1, -1, -2)
@@ -28,9 +28,13 @@
     return high, (value - high.astype(jnp.float32)).astype(jnp.bfloat16)
 
 
-def dot3(left, right):
+def products(lefts, right):
     dot = functools.partial(jnp.dot, preferred_element_type=jnp.float32)
-    return dot(left[0], right[0]) + (dot(left[0], right[1]) + dot(left[1], right[0]))
+    return [dot(left[0], right[0]) + (dot(left[0], right[1]) + dot(left[1], right[0])) for left in lefts]
+
+
+def product(left, right):
+    return products([left], right)[0]
 
 
 def invert(block):
@@ -42,8 +46,8 @@
     across = 1.0 / jnp.sum(diagonal, axis=0, keepdims=True)
     first = jnp.where(eye, 2.0 * down, 0.0) - down * block * across
     parts = split(first)
-    inner = dot3(split(block), parts)
-    return 2.0 * first - dot3(parts, split(inner))
+    inner = product(split(block), parts)
+    return 2.0 * first - product(parts, split(inner))
 
 
 def wrap(p):
@@ -220,17 +224,20 @@
         pl.semaphore_wait(barrier, greetings(STEPS1, edge1) + others)
         answer(STEPS1, edge1, ready1)
 
-    def scatter(t):
-        return remote(x_ref.at[:, :, t], rs.at[lax.rem(q, PANELS)], sc_send.at[t], sc_recv.at[lax.rem(q, PANELS)], p, 2 * t + 1)
+    def scatter(t, b):
+        k = lax.rem(q, PANELS)
+        return remote(x_ref.at[b, :, t], rs.at[k, b], sc_send.at[b, t], sc_recv.at[b, k], p, 2 * t + 1)
 
     def each_scatter(act):
         @pl.when(q < PANELS)
         def _():
-            @pl.loop(0, NC)
-            def _(t):
-                @pl.when(2 * t + 1 != q)
-                def _():
-                    act(scatter(t))
+            for b in range(2):
+
+                @pl.loop(0, NC)
+                def _(t):
+                    @pl.when(2 * t + 1 != q)
+                    def _():
+                        act(scatter(t, b))
 
     def own(half):
         piece = cols.at[1, lax.rem(p, PANELS), half]
@@ -257,6 +264,9 @@
         piece = col_piece(k, i)
         return remote(piece, piece, zc_send.at[k], zc_recv.at[k], p, partner)
 
+    def live(i):
+        return (chip > 1) | (lax.rem(i, 4) >= 2)
+
     def pass_on(k, i, act):
         away = wrap(p - k)
         for half in range(2):
@@ -273,6 +283,17 @@
         away = wrap(p - k)
         return lax.rem(i + 4 * count(away > 8), CHUNKS)
 
+    def wait_passed(first, last):
+        @pl.loop(first, last)
+        def _(i):
+            @pl.when(live(i))
+            def _():
+                for k in range(PANELS):
+
+                    @pl.when(p != k)
+                    def _():
+                        pass_on(k, in_turn(k, i), lambda copy: copy.wait_send())
+
     @pl.when(is_zero & flows)
     def _():
         mine = lax.rem(p, PANELS)
@@ -280,9 +301,9 @@
         def start_own(n, step):
             first = 0 if step == 2 else 4
 
-            @pl.when(is_root & (n < CHUNKS))
-            def _():
-                @pl.when(n >= WINDOW)
+            @pl.when(is_root & (n < CHUNKS) & live(n))
+            def _():
+                @pl.when((n >= WINDOW) & live(n + CHUNKS - WINDOW))
                 def _():
                     col_copy(mine, lax.rem(n - WINDOW + first, CHUNKS), step).wait_send()
 
@@ -316,7 +337,7 @@
                 for k in reversed(range(PANELS)):
                     away = wrap(p - k)
 
-                    @pl.when((lax.rem(away, 2) == 0) & (away != 0))
+                    @pl.when((lax.rem(away, 2) == 0) & (away != 0) & live(i))
                     def _():
                         t = in_turn(k, i)
                         col_copy(k, t, 2).wait_recv()
@@ -326,19 +347,14 @@
                         def _():
                             to_one(k, t).start()
 
-        @pl.when(is_root)
-        def _():
-            @pl.loop(CHUNKS - WINDOW, CHUNKS)
-            def _(n):
-                col_copy(mine, n, 2).wait_send()
-                col_copy(mine, lax.rem(n + 4, CHUNKS), -2).wait_send()
+        wait_passed(0, CHUNKS - 3)
 
     def await_fills():
         @pl.when(flows)
         def _():
             for k in range(PANELS):
 
-                @pl.when(lax.rem(wrap(p - k), 2) == 1)
+                @pl.when((lax.rem(wrap(p - k), 2) == 1) & (is_one | (chip > 1)))
                 def _():
                     @pl.loop(0, CHUNKS // 2)
                     def _(i):
@@ -348,9 +364,9 @@
                 def _():
                     remote(cols.at[1, k], cols.at[1, k], zc_send.at[k], zc_recv.at[k], p, partner).wait_recv()
 
-    @pl.when(jnp.logical_not(flows))
-    def _():
-        cols[...] = jnp.zeros_like(cols)
+    @pl.when((chip == 0) | ((chip == 1) & is_zero))
+    def _():
+        cols[core] = jnp.zeros_like(cols[core])
 
     def across(buffer, n, half, c):
         piece = buffer.at[half, c]
@@ -449,14 +465,16 @@
         def _():
             rs[1] = x_ref[:, :, 0]
 
-        for k in range(PANELS):
-
-            @pl.when(q != k)
-            def _():
-                remote(x_ref.at[:, :, 0], rs.at[k], sc_send.at[0], sc_recv.at[k], p, partner).wait_recv()
+        def scattered(b):
+            for k in range(PANELS):
+
+                @pl.when(q != k)
+                def _():
+                    remote(x_ref.at[b, :, 0], rs.at[k, b], sc_send.at[b, 0], sc_recv.at[b, k], p, partner).wait_recv()
 
         @pl.when(is_root)
         def _():
+            scattered(0)
             hs[mine4] = rs[:, 0]
 
         @pl.when(anchor & jnp.logical_not(is_root))
@@ -470,10 +488,14 @@
             def _():
                 along(s).start()
 
+        @pl.when(jnp.logical_not(is_root))
+        def _():
+            scattered(0)
+
+        scattered(1)
         for half in range(2):
             rows[half, chip] = rs[:, :, half]
         row_ring.begin(0)
-        row_ring.middle(0)
 
         for k in range(PANELS):
 
@@ -484,19 +506,18 @@
         for half in range(2):
             head[half, chip] = hs[:, :, half]
         head_ring.begin(0)
+        head_ring.middle(0)
+        head_ring.end(0)
+        head_ring.begin(1)
+        row_ring.middle(0)
+
+        @pl.when(is_root & flows)
+        def _():
+            cols[1, lax.rem(p, PANELS)] = x_ref[0]
+
+        head_ring.middle(1)
         row_ring.end(0)
         row_ring.begin(1)
-        head_ring.middle(0)
-        row_ring.middle(1)
-        head_ring.end(0)
-        head_ring.begin(1)
-
-        @pl.when(is_root & flows)
-        def _():
-            cols[1, lax.rem(p, PANELS)] = x_ref[0]
-
-        row_ring.end(1)
-        head_ring.middle(1)
         head_ring.end(1)
 
     @pl.when(is_zero)
@@ -512,35 +533,46 @@
         inverse = invert(a[k, k])
         fact[k, k] = inverse
         halves[k, k] = split(inverse)
-        for j in range(k + 1, PANELS):
+        below = range(k + 1, PANELS)
+        if below:
+            for i, factor in zip(below, products([split(a[i, k]) for i in below], halves[k, k])):
+                fact[i, k] = factor
+                halves[i, k] = split(factor)
+        for j in below:
             fact[k, j] = a[k, j]
             halves[k, j] = split(a[k, j])
-        for i in range(k + 1, PANELS):
-            factor = dot3(split(a[i, k]), halves[k, k])
-            fact[i, k] = factor
-            halves[i, k] = split(factor)
-            for j in range(k + 1, PANELS):
-                a[i, j] = a[i, j] - dot3(halves[i, k], halves[k, j])
+            for i, update in zip(below, products([halves[i, k] for i in below], halves[k, j])):
+                a[i, j] = a[i, j] - update
+        if k == 1:
+
+            @pl.when(is_one)
+            def _():
+                row_ring.middle(1)
 
     await_fills()
     is_panel = q < PANELS
     eye = (
         lax.broadcasted_iota(jnp.int32, (B, B), 0) == lax.broadcasted_iota(jnp.int32, (B, B), 1)
     ).astype(jnp.float32)
-    y = []
+    value = [cols[core, i].reshape(B, B) for i in range(PANELS)]
     for i in range(PANELS):
-        value = cols[core, i].reshape(B, B)
-        for k in range(i):
-            value = value - dot3(halves[i, k], y[k])
-        upper[i] = value
-        y.append(split(value))
+        upper[i] = value[i]
+        later = range(i + 1, PANELS)
+        if later:
+            for m, update in zip(later, products([halves[m, i] for m in later], split(value[i]))):
+                value[m] = value[m] - update
 
     right = [None] * PANELS
+    value = [jnp.where(is_panel, jnp.where(q == i, eye, 0.0), upper[i]) for i in range(PANELS)]
     for i in reversed(range(PANELS)):
-        value = jnp.where(is_panel, jnp.where(q == i, eye, 0.0), upper[i])
-        for k in range(i + 1, PANELS):
-            value = value - dot3(halves[i, k], right[k])
-        right[i] = split(dot3(halves[i, i], split(value)))
+        right[i] = split(product(halves[i, i], split(value[i])))
+        if i:
+            for m, update in zip(range(i), products([halves[m, i] for m in range(i)], right[i])):
+                value[m] = value[m] - update
+
+    @pl.when(is_one)
+    def _():
+        row_ring.end(1)
 
     @pl.when(is_zero)
     def _():
@@ -548,11 +580,13 @@
 
     keep = jnp.where(is_panel, 0.0, 1.0)
     sign = jnp.where(is_panel, 1.0, -1.0)
+    total = [None, None]
+    for k in range(PANELS):
+        panel = [split(rows[:, :, k, b].reshape(B, B)) for b in range(2)]
+        for b, term in enumerate(products(panel, right[k])):
+            total[b] = term if k == 0 else total[b] + term
     for b in range(2):
-        total = jnp.zeros((B, B), jnp.float32)
-        for k in range(PANELS):
-            total = total + dot3(split(rows[:, :, k, b].reshape(B, B)), right[k])
-        out_ref[b] = keep * x_ref[b].reshape(B, B) + sign * total
+        out_ref[b] = keep * x_ref[b].reshape(B, B) + sign * total[b]
 
     @pl.when(is_root & is_panel)
     def _():
@@ -566,14 +600,18 @@
 
     @pl.when(is_zero & flows)
     def _():
-        @pl.loop(0, CHUNKS)
-        def _(i):
-            for k in range(PANELS):
-
-                @pl.when(p != k)
+        @pl.when(is_root)
+        def _():
+            mine = lax.rem(p, PANELS)
+
+            @pl.loop(0, CHUNKS)
+            def _(n):
+                @pl.when(live(n) & ((n >= CHUNKS - WINDOW) | jnp.logical_not(live(n + WINDOW))))
                 def _():
-                    pass_on(k, i, lambda copy: copy.wait_send())
-
+                    col_copy(mine, n, 2).wait_send()
+                    col_copy(mine, lax.rem(n + 4, CHUNKS), -2).wait_send()
+
+        wait_passed(CHUNKS - 3, CHUNKS)
         for k in range(PANELS):
 
             @pl.when((p != k) & (lax.rem(wrap(p - k), 2) == 0))
@@ -618,8 +656,8 @@
             pltpu.VMEM((PANELS, B, B), f32),
             pltpu.SemaphoreType.REGULAR((len(STEPS0),)),
             pltpu.SemaphoreType.REGULAR((len(STEPS1),)),
-            dma((NC,)),
-            dma((PANELS,)),
+            dma((2, NC)),
+            dma((2, PANELS)),
             dma((4, 4 * SIDE)),
             dma((4, 4 * SIDE)),
             dma((len(STEPS1),)),

time: 54.8 us -> 51.6 us (0.942)
  the two profiles are of different devices: /device:TPU:227 before, /device:TPU:320 now
where the time goes in v4:
time: 51.6 us; the launch traced here: 51.4 us
  Pallas kernels  49 us (95%)
  local copies, waits for them, and re-layouts  2.41 us (5%)
    pallas_call x1, Pallas kernels, body(): pl.pallas_call(kernel, out_shape=jax.ShapeDtypeStruct((2, B, B), f32), in...  49 us
    reshape x1, local copies, waits for them, and re-layouts, body(): return out.reshape(shape)  1.33 us
    unnamed x1, local copies, waits for them, and re-layouts  1.08 us

profile of v4, /device:TPU:320, one launch (start us, length us, event | category | flops | bytes accessed | tf_op | source)
XLA Modules:
  0.0 51.4 jit_solution(2526324026808055628)
XLA Ops:
  0.0 1.1 %copy.3 = f32[2,1,256,1,256]{4,2,3,1,0:T(8,128)S(1)} copy(f32[2,1,256,1,256]{4,3,2,1,0:T(1,128)} %param.1) | data formatting | bytes 1048576
  1.1 49.0 %shard_map.17 = f32[2,256,256]{2,1,0:T(8,128)S(1)} custom-call(f32[2,2,16,8,256]{4,3,2,1,0:T(8,128)S(1)} %bitcast.3), custom_call_target="tpu_custom_call" | custom-call | tf_op jit(solution)/shard_map/pallas_call | solution.py:644
  50.1 1.3 %copy.2 = f32[2,1,256,1,256]{4,3,2,1,0:T(1,128)} copy(f32[2,1,256,1,256]{4,2,0,3,1:T(8,128)S(1)} %bitcast.2) | data formatting | bytes 1048576 | tf_op jit(solution)/shard_map/reshape | solution.py:680

commit v5 on v4

--- a/solution.py
+++ b/solution.py
@@ -85,6 +85,8 @@
 
 
 def kernel(
+    x_hbm,
+    out_hbm,
     x_ref,
     out_ref,
     rs,
@@ -96,15 +98,14 @@
     upper,
     ready0,
     ready1,
+    io,
     sc_send,
     sc_recv,
-    ra_send,
+    sends,
     ra_recv,
+    ha_recv,
     hz_send,
     hz_recv,
-    ha_send,
-    ha_recv,
-    z_send,
     z_recv,
     own_send,
     own_recv,
@@ -136,6 +137,9 @@
     def count(flag):
         return flag.astype(jnp.int32)
 
+    fetch = pltpu.make_async_copy(x_hbm, x_ref, io.at[0])
+    fetch.start()
+
     barrier = pltpu.get_barrier_semaphore()
 
     def greet(steps, edge):
@@ -224,20 +228,11 @@
         pl.semaphore_wait(barrier, greetings(STEPS1, edge1) + others)
         answer(STEPS1, edge1, ready1)
 
+    fetch.wait()
+
     def scatter(t, b):
         k = lax.rem(q, PANELS)
-        return remote(x_ref.at[b, :, t], rs.at[k, b], sc_send.at[b, t], sc_recv.at[b, k], p, 2 * t + 1)
-
-    def each_scatter(act):
-        @pl.when(q < PANELS)
-        def _():
-            for b in range(2):
-
-                @pl.loop(0, NC)
-                def _(t):
-                    @pl.when(2 * t + 1 != q)
-                    def _():
-                        act(scatter(t, b))
+        return remote(x_ref.at[b, :, t], rs.at[k, b], sc_send.at[b], sc_recv.at[b, k], p, 2 * t + 1)
 
     def own(half):
         piece = cols.at[1, lax.rem(p, PANELS), half]
@@ -248,17 +243,26 @@
         own(0).start()
         own(1).start()
 
-    each_scatter(lambda copy: copy.start())
+    @pl.when(q < PANELS)
+    def _():
+        for b in range(2):
+
+            @pl.loop(0, NC)
+            def _(t):
+                @pl.when(2 * t + 1 != q)
+                def _():
+                    scatter(t, b).start()
 
     def col_piece(k, i):
         half, j = i // 4, lax.rem(i, 4)
         return cols.at[j // 2, k, half, pl.ds(lax.rem(j, 2) * (CR // S), CR // S)]
 
-    def col_copy(k, i, step):
+    def col_copy(k, half, i, step, slot=None):
         piece = col_piece(k, i)
         n = STEPS0.index(step)
         to = q + lax.rem(i, 4) // 2 if step in (1, -1) else q
-        return remote(piece, piece, z_send.at[n, k * CHUNKS + i], z_recv.at[k * CHUNKS + i], wrap(p + step), to)
+        send = sends.at[(k * 2 + half) * 4 + n if slot is None else slot]
+        return remote(piece, piece, send, z_recv.at[k * CHUNKS + i], wrap(p + step), to)
 
     def to_one(k, i):
         piece = col_piece(k, i)
@@ -267,7 +271,7 @@
     def live(i):
         return (chip > 1) | (lax.rem(i, 4) >= 2)
 
-    def pass_on(k, i, act):
+    def pass_on(k, i):
         away = wrap(p - k)
         for half in range(2):
 
@@ -277,37 +281,39 @@
 
                     @pl.when(among(away, ON[half][s]))
                     def _():
-                        act(col_copy(k, i, s))
+                        col_copy(k, half, i, s).start()
+
+    def passed(k):
+        away = wrap(p - k)
+        for half in range(2):
+            for n, s in enumerate(STEPS0):
+                places = among(away, ON[half][s])
+                for flag, piece in ((chip > 1, cols.at[:, k, half]), (chip == 1, cols.at[1, k, half])):
+
+                    @pl.when(places & flag)
+                    def _():
+                        remote(piece, piece, sends.at[(k * 2 + half) * 4 + n], z_recv.at[0], p, partner).wait_send()
 
     def in_turn(k, i):
         away = wrap(p - k)
         return lax.rem(i + 4 * count(away > 8), CHUNKS)
 
-    def wait_passed(first, last):
-        @pl.loop(first, last)
-        def _(i):
-            @pl.when(live(i))
-            def _():
-                for k in range(PANELS):
-
-                    @pl.when(p != k)
-                    def _():
-                        pass_on(k, in_turn(k, i), lambda copy: copy.wait_send())
-
     @pl.when(is_zero & flows)
     def _():
         mine = lax.rem(p, PANELS)
 
+        def own_copy(n, step):
+            i = lax.rem(n + (0 if step == 2 else 4), CHUNKS)
+            return col_copy(mine, 0, i, step, 6 * 4 + (0 if step == 2 else WINDOW) + lax.rem(n, WINDOW))
+
         def start_own(n, step):
-            first = 0 if step == 2 else 4
-
             @pl.when(is_root & (n < CHUNKS) & live(n))
             def _():
                 @pl.when((n >= WINDOW) & live(n + CHUNKS - WINDOW))
                 def _():
-                    col_copy(mine, lax.rem(n - WINDOW + first, CHUNKS), step).wait_send()
-
-                col_copy(mine, lax.rem(n + first, CHUNKS), step).start()
+                    own_copy(n - WINDOW, step).wait_send()
+
+                own_copy(n, step).start()
 
         @pl.when(is_root)
         def _():
@@ -340,14 +346,21 @@
                     @pl.when((lax.rem(away, 2) == 0) & (away != 0) & live(i))
                     def _():
                         t = in_turn(k, i)
-                        col_copy(k, t, 2).wait_recv()
-                        pass_on(k, t, lambda copy: copy.start())
+                        col_copy(k, 0, t, 2).wait_recv()
+                        pass_on(k, t)
 
                         @pl.when(lax.rem(t, 4) >= 2)
                         def _():
                             to_one(k, t).start()
 
-        wait_passed(0, CHUNKS - 3)
+        @pl.when(is_root)
+        def _():
+            @pl.loop(0, CHUNKS)
+            def _(n):
+                @pl.when(live(n) & ((n >= CHUNKS - WINDOW) | jnp.logical_not(live(n + WINDOW))))
+                def _():
+                    own_copy(n, 2).wait_send()
+                    own_copy(n, -2).wait_send()
 
     def await_fills():
         @pl.when(flows)
@@ -358,7 +371,7 @@
                 def _():
                     @pl.loop(0, CHUNKS // 2)
                     def _(i):
-                        col_copy(k, (i // 2) * 4 + core * 2 + lax.rem(i, 2), 2).wait_recv()
+                        col_copy(k, 0, (i // 2) * 4 + core * 2 + lax.rem(i, 2), 2).wait_recv()
 
                 @pl.when(is_one & (p != k) & (lax.rem(wrap(p - k), 2) == 0))
                 def _():
@@ -376,8 +389,8 @@
         return remote(buffer, buffer, cc_send.at[n], cc_recv.at[n], p, partner)
 
     class Ring:
-        def __init__(self, buffer, send, recv, n):
-            self.buffer, self.send, self.recv, self.n = buffer, send, recv, n
+        def __init__(self, buffer, recv, n, apart):
+            self.buffer, self.recv, self.n, self.apart = buffer, recv, n, apart
 
         def line(self, stage, half, t, step):
             if stage == half:
@@ -396,8 +409,20 @@
             piece = self.buffer.at[half, self.line(stage, half, t, 0 if kind < 2 else -step)]
             if kind >= 2:
                 piece = piece.at[:, :, :, pl.ds((kind - 2) * (B // 2), B // 2)]
-            i = (stage * SIDE + t) * 2 + half
-            return remote(piece, piece, self.send.at[kind, i], self.recv.at[kind, i], p, self.neighbour(stage, half, step))
+            return self.between(piece, stage, half, t, kind, self.neighbour(stage, half, step))
+
+        def between(self, piece, stage, half, t, kind, to):
+            i = kind * 4 + stage * 2 + half
+            recv = self.recv.at[i]
+            if self.apart and stage == 1 and kind < 2:
+                recv = self.recv.at[16 + (kind * 2 + half) * SIDE + t]
+            return remote(piece, piece, sends.at[self.n * 16 + i], recv, p, to)
+
+        def all_of(self, stage, half, kind):
+            piece = self.buffer.at[half, pl.ds(0, SIDE if stage else 1)]
+            if kind >= 2:
+                piece = piece.at[:, :, :, :, pl.ds(0, B // 2)]
+            return self.between(piece, stage, half, 0, kind, partner)
 
         def each(self, stage, act):
             if stage == 0:
@@ -423,30 +448,32 @@
             self.each(stage, act)
 
         def middle(self, stage):
+            apart = self.apart and stage == 1
+            if not apart:
+                for half in range(2):
+                    for kind in range(2):
+                        self.all_of(stage, half, kind).wait_recv()
+
             def act(half, t):
                 for kind in range(2):
-                    self.copy(stage, half, t, kind).wait_recv()
+                    if apart:
+                        self.copy(stage, half, t, kind).wait_recv()
                     self.copy(stage, half, t, 2 + kind).start()
                     self.push(stage, half, t, -1 if kind == 0 else 1)
 
             self.each(stage, act)
 
         def end(self, stage):
-            def act(half, t):
+            for half in range(2):
                 for kind in (2, 3):
-                    self.copy(stage, half, t, kind).wait_recv()
-                self.push(stage, half, t, 2)
-
-            self.each(stage, act)
+                    self.all_of(stage, half, kind).wait_recv()
+            self.each(stage, lambda half, t: self.push(stage, half, t, 2))
 
         def sent(self):
             for stage in range(2):
-
-                def act(half, t):
+                for half in range(2):
                     for kind in range(4):
-                        self.copy(stage, half, t, kind).wait_send()
-
-                self.each(stage, act)
+                        self.all_of(stage, half, kind).wait_send()
 
     near = lax.rem(p, 4)
     mine4 = lax.rem(near, PANELS)
@@ -456,8 +483,8 @@
         n = STEPS1.index(step)
         return remote(hs.at[mine4], hs.at[mine4], hz_send.at[n], hz_recv.at[mine4], wrap(p + step), q)
 
-    row_ring = Ring(rows, ra_send, ra_recv, 0)
-    head_ring = Ring(head, ha_send, ha_recv, 1)
+    row_ring = Ring(rows, ra_recv, 0, False)
+    head_ring = Ring(head, ha_recv, 1, True)
 
     @pl.when(is_one)
     def _():
@@ -470,7 +497,7 @@
 
                 @pl.when(q != k)
                 def _():
-                    remote(x_ref.at[b, :, 0], rs.at[k, b], sc_send.at[b, 0], sc_recv.at[b, k], p, partner).wait_recv()
+                    remote(x_ref.at[b, :, 0], rs.at[k, b], sc_send.at[b], sc_recv.at[b, k], p, partner).wait_recv()
 
         @pl.when(is_root)
         def _():
@@ -585,34 +612,41 @@
         panel = [split(rows[:, :, k, b].reshape(B, B)) for b in range(2)]
         for b, term in enumerate(products(panel, right[k])):
             total[b] = term if k == 0 else total[b] + term
+    def store(b):
+        return pltpu.make_async_copy(out_ref.at[b], out_hbm.at[b], io.at[1 + b])
+
+    out_ref[1] = keep * x_ref[1].reshape(B, B) + sign * total[1]
+    store(1).start()
+
+    @pl.when(jnp.logical_not(is_root))
+    def _():
+        out_ref[0] = keep * x_ref[0].reshape(B, B) + sign * total[0]
+
+    @pl.when(is_root & is_panel)
+    def _():
+        out_ref[0] = fact[lax.rem(p, PANELS), lax.rem(q, PANELS)]
+
+    @pl.when(is_root & (q >= PANELS))
+    def _():
+        out_ref[0] = upper[lax.rem(p, PANELS)]
+
+    store(0).start()
+
     for b in range(2):
-        out_ref[b] = keep * x_ref[b].reshape(B, B) + sign * total[b]
-
-    @pl.when(is_root & is_panel)
-    def _():
-        out_ref[0] = fact[lax.rem(p, PANELS), lax.rem(q, PANELS)]
-
-    @pl.when(is_root & (q >= PANELS))
-    def _():
-        out_ref[0] = upper[lax.rem(p, PANELS)]
-
-    each_scatter(lambda copy: copy.wait_send())
+        for pieces, flag in ((NC - 1, q == 1), (NC, scatters)):
+
+            @pl.when(flag)
+            def _():
+                piece = x_ref.at[b, :, pl.ds(0, pieces)]
+                remote(piece, piece, sc_send.at[b], sc_recv.at[b, 0], p, partner).wait_send()
 
     @pl.when(is_zero & flows)
     def _():
-        @pl.when(is_root)
-        def _():
-            mine = lax.rem(p, PANELS)
-
-            @pl.loop(0, CHUNKS)
-            def _(n):
-                @pl.when(live(n) & ((n >= CHUNKS - WINDOW) | jnp.logical_not(live(n + WINDOW))))
-                def _():
-                    col_copy(mine, n, 2).wait_send()
-                    col_copy(mine, lax.rem(n + 4, CHUNKS), -2).wait_send()
-
-        wait_passed(CHUNKS - 3, CHUNKS)
         for k in range(PANELS):
+
+            @pl.when(p != k)
+            def _():
+                passed(k)
 
             @pl.when((p != k) & (lax.rem(wrap(p - k), 2) == 0))
             def _():
@@ -635,6 +669,9 @@
         head_ring.sent()
         whole(rows, 0).wait_send()
         whole(head, 1).wait_send()
+
+    store(0).wait()
+    store(1).wait()
 
 
 def body(matrix):
@@ -644,9 +681,11 @@
     out = pl.pallas_call(
         kernel,
         out_shape=jax.ShapeDtypeStruct((2, B, B), f32),
-        in_specs=[pl.BlockSpec(memory_space=pltpu.VMEM)],
-        out_specs=pl.BlockSpec(memory_space=pltpu.VMEM),
+        in_specs=[pl.BlockSpec(memory_space=pl.ANY)],
+        out_specs=pl.BlockSpec(memory_space=pl.ANY),
         scratch_shapes=[
+            pltpu.VMEM((2, 2, NC, S, B), f32),
+            pltpu.VMEM((2, B, B), f32),
             pltpu.VMEM((PANELS, 2, 2, S, B), f32),
             pltpu.VMEM((2, NC, PANELS, 2, S, B), f32),
             pltpu.VMEM((PANELS, PANELS, 2, S, B), f32),
@@ -656,15 +695,14 @@
             pltpu.VMEM((PANELS, B, B), f32),
             pltpu.SemaphoreType.REGULAR((len(STEPS0),)),
             pltpu.SemaphoreType.REGULAR((len(STEPS1),)),
-            dma((2, NC)),
+            dma((3,)),
+            dma((2,)),
             dma((2, PANELS)),
-            dma((4, 4 * SIDE)),
-            dma((4, 4 * SIDE)),
+            dma((32,)),
+            dma((16,)),
+            dma((32,)),
             dma((len(STEPS1),)),
             dma((PANELS,)),
-            dma((4, 4 * SIDE)),
-            dma((4, 4 * SIDE)),
-            dma((len(STEPS0), PANELS * CHUNKS)),
             dma((PANELS * CHUNKS,)),
             dma((2,)),
             dma((2,)),

time: 51.6 us -> 49.5 us (0.959)
  Pallas kernels: 49 us -> 46.9 us
    pallas_call x1, Pallas kernels: 49 us -> 46.9 us  [body(): pl.pallas_call(kernel, out_shape=jax.ShapeDtypeStruct((2, B, B), f32), in...]
where the time goes in v5:
time: 49.5 us; the launch traced here: 49.4 us
  Pallas kernels  46.9 us (95%)
  local copies, waits for them, and re-layouts  2.41 us (5%)
    pallas_call x1, Pallas kernels, body(): pl.pallas_call(kernel, out_shape=jax.ShapeDtypeStruct((2, B, B), f32), in...  46.9 us
    reshape x1, local copies, waits for them, and re-layouts, body(): return out.reshape(shape)  1.33 us
    unnamed x1, local copies, waits for them, and re-layouts  1.08 us

profile of v5, /device:TPU:320, one launch (start us, length us, event | category | flops | bytes accessed | tf_op | source)
XLA Modules:
  0.0 49.4 jit_solution(9579745432830977061)
XLA Ops:
  0.0 1.1 %copy.3 = f32[2,1,256,1,256]{4,2,3,1,0:T(8,128)S(1)} copy(f32[2,1,256,1,256]{4,3,2,1,0:T(1,128)} %param.1) | data formatting | bytes 1048576
  1.1 46.9 %shard_map.17 = f32[2,256,256]{2,1,0:T(8,128)S(1)} custom-call(f32[2,2,16,8,256]{4,3,2,1,0:T(8,128)S(1)} %bitcast.3), custom_call_target="tpu_custom_call" | custom-call | tf_op jit(solution)/shard_map/pallas_call | solution.py:681
  48.0 1.3 %copy.2 = f32[2,1,256,1,256]{4,3,2,1,0:T(1,128)} copy(f32[2,1,256,1,256]{4,2,0,3,1:T(8,128)S(1)} %bitcast.2) | data formatting | bytes 1048576 | tf_op jit(solution)/shard_map/reshape | solution.py:718

commit v6 on v5

--- a/solution.py
+++ b/solution.py
@@ -63,7 +63,7 @@
 
 ON = (
     {2: (0, 2, 4, 6, 8), -2: (0, 14), -1: (2, 4, 6, 8, 10), 1: (10, 12, 14)},
-    {2: (0, 2, 4), -2: (0, 14, 12, 10), -1: (2, 4, 6, 8), 1: (8, 10, 12, 14)},
+    {2: (0, 2, 4), -2: (0, 14, 12, 10), -1: (2, 4, 6), 1: (6, 8, 10, 12, 14)},
 )
 
 
@@ -424,28 +424,22 @@
                 piece = piece.at[:, :, :, :, pl.ds(0, B // 2)]
             return self.between(piece, stage, half, 0, kind, partner)
 
-        def each(self, stage, act):
-            if stage == 0:
+        def each(self, stage, act, offsets=(0, 1, 3, 2)):
+            for offset in offsets if stage else (0,):
                 for half in range(2):
-                    act(half, 0)
-                return
-
-            @pl.loop(0, SIDE)
-            def _(t):
-                for half in range(2):
-                    act(half, t)
+                    act(half, lax.rem((chip_y if half else chip_x) + offset, SIDE) if stage else 0)
 
         def push(self, stage, half, t, step):
             if stage == 1:
                 across(self.buffer, self.n, half, self.line(stage, half, t, step)).start()
 
-        def begin(self, stage):
+        def begin(self, stage, offsets=(0, 1, 3, 2)):
             def act(half, t):
                 self.copy(stage, half, t, 0).start()
                 self.copy(stage, half, t, 1).start()
                 self.push(stage, half, t, 0)
 
-            self.each(stage, act)
+            self.each(stage, act, offsets)
 
         def middle(self, stage):
             apart = self.apart and stage == 1
@@ -533,9 +527,11 @@
         for half in range(2):
             head[half, chip] = hs[:, :, half]
         head_ring.begin(0)
+        head_ring.begin(1, (0,))
         head_ring.middle(0)
+        head_ring.begin(1, (1, 3))
         head_ring.end(0)
-        head_ring.begin(1)
+        head_ring.begin(1, (2,))
         row_ring.middle(0)
 
         @pl.when(is_root & flows)

time: 49.5 us -> 48.1 us (0.972)
  the two profiles are of different devices: /device:TPU:320 before, /device:TPU:238 now
where the time goes in v6:
time: 48.1 us; the launch traced here: 48 us
  Pallas kernels  45.5 us (95%)
  local copies, waits for them, and re-layouts  2.41 us (5%)
    pallas_call x1, Pallas kernels, body(): pl.pallas_call(kernel, out_shape=jax.ShapeDtypeStruct((2, B, B), f32), in...  45.5 us
    reshape x1, local copies, waits for them, and re-layouts, body(): return out.reshape(shape)  1.33 us
    unnamed x1, local copies, waits for them, and re-layouts  1.08 us

profile of v6, /device:TPU:238, one launch (start us, length us, event | category | flops | bytes accessed | tf_op | source)
XLA Modules:
  0.0 48.0 jit_solution(6862163358071081997)
XLA Ops:
  0.0 1.1 %copy.3 = f32[2,1,256,1,256]{4,2,3,1,0:T(8,128)S(1)} copy(f32[2,1,256,1,256]{4,3,2,1,0:T(1,128)} %param.1) | data formatting | bytes 1048576
  1.1 45.5 %shard_map.17 = f32[2,256,256]{2,1,0:T(8,128)S(1)} custom-call(f32[2,2,16,8,256]{4,3,2,1,0:T(8,128)S(1)} %bitcast.3), custom_call_target="tpu_custom_call" | custom-call | tf_op jit(solution)/shard_map/pallas_call | solution.py:677
  46.6 1.3 %copy.2 = f32[2,1,256,1,256]{4,3,2,1,0:T(1,128)} copy(f32[2,1,256,1,256]{4,2,0,3,1:T(8,128)S(1)} %bitcast.2) | data formatting | bytes 1048576 | tf_op jit(solution)/shard_map/reshape | solution.py:714

commit v7 on v6

--- a/solution.py
+++ b/solution.py
@@ -17,7 +17,7 @@
 CHUNKS = 8
 CR = 2 * B // CHUNKS
 WINDOW = 2
-LAG = 3
+LAG = 4
 MESH = pl.DeviceIdType.MESH
 STEPS0 = (2, 1, -1, -2)
 STEPS1 = (4, 1, -1, -2, -4)

time: 48.1 us -> 49.8 us (1.035)
  Pallas kernels: 45.5 us -> 47.3 us
    pallas_call x1, Pallas kernels: 45.5 us -> 47.3 us  [body(): pl.pallas_call(kernel, out_shape=jax.ShapeDtypeStruct((2, B, B), f32), in...]
where the time goes in v7:
time: 49.8 us; the launch traced here: 49.7 us
  Pallas kernels  47.3 us (95%)
  local copies, waits for them, and re-layouts  2.41 us (5%)
    pallas_call x1, Pallas kernels, body(): pl.pallas_call(kernel, out_shape=jax.ShapeDtypeStruct((2, B, B), f32), in...  47.3 us
    reshape x1, local copies, waits for them, and re-layouts, body(): return out.reshape(shape)  1.33 us
    unnamed x1, local copies, waits for them, and re-layouts  1.08 us

profile of v7, /device:TPU:238, one launch (start us, length us, event | category | flops | bytes accessed | tf_op | source)
XLA Modules:
  0.0 49.7 jit_solution(11224508387381774892)
XLA Ops:
  0.0 1.1 %copy.3 = f32[2,1,256,1,256]{4,2,3,1,0:T(8,128)S(1)} copy(f32[2,1,256,1,256]{4,3,2,1,0:T(1,128)} %param.1) | data formatting | bytes 1048576
  1.1 47.3 %shard_map.17 = f32[2,256,256]{2,1,0:T(8,128)S(1)} custom-call(f32[2,2,16,8,256]{4,3,2,1,0:T(8,128)S(1)} %bitcast.3), custom_call_target="tpu_custom_call" | custom-call | tf_op jit(solution)/shard_map/pallas_call | solution.py:677
  48.4 1.3 %copy.2 = f32[2,1,256,1,256]{4,3,2,1,0:T(1,128)} copy(f32[2,1,256,1,256]{4,2,0,3,1:T(8,128)S(1)} %bitcast.2) | data formatting | bytes 1048576 | tf_op jit(solution)/shard_map/reshape | solution.py:714
